TPU v7x, 128 devices: a whole 4x4x4 slice. The times are simulated.
128 devices in a mesh: seq: 16 (over z, y), expert: 8 (over x, core).
Axes of the slice: x: 4, y: 4, z: 4, core: 2. Of those that a mesh axis runs over, the one named last changes fastest.
Arguments:
- tokens: bfloat16 [2048, 4096], P(('seq', 'expert')), may hold values from -6 to 6
- gain_mamba: float32 [4096], replicated, may hold values from 0.1 to 1.9
- in_weight: bfloat16 [2, 4096, 8192], P(None, 'seq', 'expert'), may hold values from -0.09375 to 0.09375
- conv_weight: float32 [4, 8192], P(None, 'expert'), may hold values from -3 to 3
- conv_bias: float32 [8192], P('expert'), may hold values from -3 to 3
- xproj_weight: bfloat16 [8192, 288], P('expert'), may hold values from -0.0625 to 0.0625
- dt_weight: bfloat16 [256, 8192], P(None, 'expert'), may hold values from -0.375 to 0.375
- dt_bias: float32 [8192], P('expert'), may hold values from -7 to -2
- a_rate: float32 [16, 8192], P(None, 'expert'), may hold values from 0.01 to 8
- skip_d: float32 [8192], P('expert'), may hold values from 0.5 to 1.5
- out_weight: bfloat16 [8192, 4096], P('expert', 'seq'), may hold values from -0.0625 to 0.0625
- gain_moe: float32 [4096], replicated, may hold values from 0.1 to 1.9
- expert_ids: int32 [2048, 2], P(('seq', 'expert')), may hold values from 0 to 15, all different within a row; in each aligned block of 16 rows (0 to 15, 16 to 31, ...) at most 4 rows name the same one
- gate_weights: float32 [2048, 2], P(('seq', 'expert')), may hold values from 0.2 to 1
- w_gate: bfloat16 [16, 4096, 7168], P('seq', None, 'expert'), may hold values from -0.09375 to 0.09375
- w_up: bfloat16 [16, 4096, 7168], P('seq', None, 'expert'), may hold values from -0.09375 to 0.09375
- w_down: bfloat16 [16, 7168, 4096], P('seq', 'expert'), may hold values from -0.0625 to 0.0625
Outputs:
- mixed: bfloat16 [2048, 4096], P(('seq', 'expert'))
Inputs may be any that keep to these rules, and one draw needn't show every extreme that they name: `expert_ids`: each row names 2 different experts. In each aligned block of 16 rows (the rows of one device) no expert is named by more than 4 rows, a bound that some block reaches.
All inputs are finite; a program needn't handle non-finite values.
Results may differ from a plain program's by a relative error of at most 0.03.
Values may be sent and summed in bfloat16 or wider, within the bound.
A program may use at most 192 MiB of HBM per device.

v0:
```python
import jax
import jax.numpy as jnp
from jax import lax
from jax.sharding import PartitionSpec as P

STATE = 16
CONV = 4
RANK = 256
TOP = 2


def from_behind(block, axis, distance):
    devices = range(lax.axis_size(axis))
    route = [(i - distance, i) for i in devices if i - distance in devices]
    return lax.ppermute(block, axis, route)


def rms_norm(values, gain):
    wide = values.astype(jnp.float32)
    return wide * lax.rsqrt(jnp.mean(wide * wide, axis=-1, keepdims=True) + 1e-05) * gain


def combine_states(earlier, later):
    return (earlier[0] * later[0], later[0] * earlier[1] + later[1])


def per_device(
    tokens,
    gain_mamba,
    in_weight,
    conv_weight,
    conv_bias,
    xproj_weight,
    dt_weight,
    dt_bias,
    a_rate,
    skip_d,
    out_weight,
    gain_moe,
    expert_ids,
    gate_weights,
    w_gate,
    w_up,
    w_down,
):
    rows, dim = tokens.shape
    n_seq = lax.axis_size("seq")
    n_exp = lax.axis_size("expert")
    group = lax.all_gather(tokens, "expert", axis=0, tiled=True)
    local_tok = group.shape[0]
    normed = rms_norm(group, gain_mamba).astype(jnp.bfloat16)
    both = jnp.einsum(
        "td,kdc->tkc",
        normed,
        lax.all_gather(in_weight, "seq", axis=1, tiled=True),
        preferred_element_type=jnp.float32,
    )
    xpart = both[:, 0]
    zpart = both[:, 1]
    edge = from_behind(xpart[local_tok - (CONV - 1) :], "seq", 1)
    padded = jnp.concatenate([edge, xpart], axis=0)
    conv = conv_bias
    for tap in range(CONV):
        conv = conv + conv_weight[tap] * padded[tap : tap + local_tok]
    inner = jax.nn.silu(conv).astype(jnp.bfloat16)
    partial_value = jnp.dot(inner, xproj_weight, preferred_element_type=jnp.float32)
    low_part, edge_part = (
        lax.psum(partial_value[:, :RANK].astype(jnp.bfloat16), "expert").astype(jnp.float32),
        lax.psum(partial_value[:, RANK:].astype(jnp.bfloat16), "expert").astype(jnp.float32),
    )
    dt_low = low_part.astype(jnp.bfloat16)
    bmat = edge_part[:, :STATE]
    cmat = edge_part[:, STATE:]
    step = jax.nn.softplus(jnp.dot(dt_low, dt_weight, preferred_element_type=jnp.float32) + dt_bias)
    inner_f = inner.astype(jnp.float32)
    decay = jnp.exp(-step[:, None, :] * a_rate[None, :, :])
    source = bmat[:, :, None] * (step * inner_f)[:, None, :]
    cumulative, states = lax.associative_scan(combine_states, (decay, source), axis=0)
    total = cumulative[-1]
    final = states[-1]

    def relay(turn, incoming):
        return from_behind((total * incoming + final).astype(jnp.bfloat16), "seq", 1).astype(
            jnp.float32
        )

    arriving = lax.fori_loop(0, n_seq - 1, relay, jnp.zeros_like(final))
    states = states + cumulative * arriving[None, :, :]
    readout = jnp.sum(cmat[:, :, None] * states, axis=1)
    gated = ((readout + skip_d * inner_f) * jax.nn.silu(zpart)).astype(jnp.bfloat16)
    terms = jnp.dot(
        gated,
        lax.all_gather(out_weight, "seq", axis=1, tiled=True),
        preferred_element_type=jnp.float32,
    )
    mixer = lax.psum_scatter(
        terms.astype(jnp.bfloat16), "expert", scatter_dimension=0, tiled=True
    ).astype(jnp.float32)
    resid = (tokens.astype(jnp.float32) + mixer).astype(jnp.bfloat16)
    normed2 = rms_norm(resid, gain_moe).astype(jnp.bfloat16)
    capacity = max(2, 4 * rows // n_seq)
    slots_all = n_seq * capacity
    flat_ids = expert_ids.reshape(-1)
    onehot = (flat_ids[:, None] == jnp.arange(n_seq, dtype=jnp.int32)[None, :]).astype(jnp.int32)
    before = jnp.cumsum(onehot, axis=0) - onehot
    slot = jnp.sum(before * onehot, axis=1)
    target = flat_ids * capacity + slot
    places = target[:, None] == jnp.arange(slots_all, dtype=jnp.int32)[None, :]
    dispatch_mat = jnp.any(places.reshape(rows, TOP, slots_all), axis=1).astype(jnp.bfloat16)
    send = jnp.einsum(
        "rp,rd->pd", dispatch_mat, normed2, preferred_element_type=jnp.float32
    ).astype(jnp.bfloat16)
    received = lax.all_to_all(
        send.reshape(n_seq, capacity, dim), "seq", split_axis=0, concat_axis=0, tiled=True
    )
    pooled = lax.all_gather(
        received.reshape(1, slots_all, dim), "expert", axis=0, tiled=True
    ).reshape(n_exp * slots_all, dim)
    gate = jnp.dot(pooled, w_gate[0], preferred_element_type=jnp.float32)
    upper = jnp.dot(pooled, w_up[0], preferred_element_type=jnp.float32)
    act = (jax.nn.silu(gate) * upper).astype(jnp.bfloat16)
    outputs = lax.psum_scatter(
        jnp.dot(act, w_down[0], preferred_element_type=jnp.float32).astype(jnp.bfloat16),
        "expert",
        scatter_dimension=0,
        tiled=True,
    )
    returned = lax.all_to_all(
        outputs.reshape(n_seq, capacity, dim), "seq", split_axis=0, concat_axis=0, tiled=True
    ).reshape(slots_all, dim)
    weighting = jnp.where(places, gate_weights.reshape(-1)[:, None], 0.0)
    weighting = jnp.sum(weighting.reshape(rows, TOP, slots_all), axis=1)
    moe = jnp.dot(weighting, returned.astype(jnp.float32), precision=lax.Precision.HIGHEST)
    return (resid.astype(jnp.float32) + moe).astype(jnp.bfloat16)


def solution(mesh):
    placed = (
        P(("seq", "expert"), None),
        P(),
        P(None, "seq", "expert"),
        P(None, "expert"),
        P("expert"),
        P("expert", None),
        P(None, "expert"),
        P("expert"),
        P(None, "expert"),
        P("expert"),
        P("expert", "seq"),
        P(),
        P(("seq", "expert"), None),
        P(("seq", "expert"), None),
        P("seq", None, "expert"),
        P("seq", None, "expert"),
        P("seq", "expert", None),
    )
    return jax.shard_map(
        per_device,
        mesh=mesh,
        in_specs=placed,
        out_specs=P(("seq", "expert"), None),
        check_vma=False,
    )
```

profile of v0, /device:TPU:0, one launch (start us, length us, event | category | flops | bytes accessed | tf_op | source)
XLA Modules:
  0.0 908.5 jit_solution(7577490913799089768)
XLA Ops:
  8.9 26.0 %all-gather.5.cloned.1.call-done = bf16[128,4096]{1,0:T(8,128)(2,1)} async-done(((bf16[16,4096]{1,0:T(8,128)(2,1)}), bf16[128,4096]{1,0:T(8,128)(2,1)}) %all-gather.5.cloned.1.call-update) | async-done | bytes 1048592 | tf_op jit(solution)/shard_map/all_gather | solution.py:49
  36.5 111.9 %all-gather.7.cloned.1.call-done = bf16[2,4096,1024]{2,1,0:T(8,128)(2,1)} async-done(((bf16[2,256,1024]{2,1,0:T(8,128)(2,1)}), bf16[2,4096,1024]{2,1,0:T(8,128)(2,1)}) %all-gather.7.cloned.1.call-update) | async-done | bytes 16777232 | tf_op jit(solution)/shard_map/all_gather | solution.py:55
  148.4 8.5 fusion.20
  156.9 3.5 collective-permute-start.1
  163.9 14.0 %psum.14 = bf16[128,32]{0,1:T(8,128)(2,1)S(1)} all-reduce(bf16[128,32]{0,1:T(8,128)(2,1)S(1)} %slice.341), channel_id=1, replica_groups=mesh['seq'=16,'expert'=8] {'expert'}, use_global_device_ids=true, to_apply=%region_1.2 | all-reduce | flops 4096 | bytes 16384 | tf_op jit(solution)/shard_map/psum | solution.py:69
  178.7 44.8 %all-reduce.30.cloned.1.call-done = bf16[128,256]{0,1:T(8,128)(2,1)} async-done(((bf16[128,256]{0,1:T(8,128)(2,1)}), bf16[128,256]{0,1:T(8,128)(2,1)}) %all-reduce.30.cloned.1.call-update) | async-done | bytes 65552 | tf_op jit(solution)/shard_map/psum | solution.py:68
  227.0 3.3 copy-done.3
  233.5 10.9 %slice_add_fusion = (f32[64,16,1024]{2,1,0:T(8,128)S(1)}, f32[64,16,1024]{2,1,0:T(8,128)}) fusion(f32[128,16,1024]{2,1,0:T(8,128)} %copy-done.3, f32[128,16,1024]{2,1,0:T(8,128)} %copy-done.2), kind=kLoop, calls=%fused_computation.19 | loop fusion | flops 3145728 | bytes 25165824 | tf_op jit(solution)/shard_map/add | solution.py:24
  246.6 3.3 slice_add_fusion.1
  258.9 2.2 pad.103
  262.7 2.2 pad.88
  266.4 2.2 pad.89
  276.6 3.7 pad.91
  288.7 3.5 pad.107
  293.3 3.5 pad.92
  296.8 3.5 pad.93
  301.5 2.7 add.253
  304.2 3.1 fusion.24
  308.4 7.0 pad.108
  315.3 10.2 %pad.109 = f32[32,16,1024]{2,1,0:T(8,128)} pad(f32[16,16,1024]{2,1,0:T(8,128)} %add.263, f32[]{:T(128)} %constant.13.clone.1), padding=1_0_1x0_0_0x0_0_0 | pad | bytes 3145732 | tf_op jit(solution)/shard_map/pad | solution.py:78
  325.5 10.1 %pad.95 = f32[32,16,1024]{2,1,0:T(8,128)} pad(f32[16,16,1024]{2,1,0:T(8,128)} %add.253, f32[]{:T(128)} %constant.13.clone.1), padding=1_0_1x0_0_0x0_0_0 | pad | bytes 3145732 | tf_op jit(solution)/shard_map/pad | solution.py:78
  335.6 2.3 pad_maximum_fusion.4
  337.9 10.2 %pad.94 = f32[32,16,1024]{2,1,0:T(8,128)} pad(f32[16,16,1024]{2,1,0:T(8,128)} %pad_maximum_fusion.4, f32[]{:T(128)} %constant.13.clone.1), padding=0_1_1x0_0_0x0_0_0 | pad | bytes 3145732 | tf_op jit(solution)/shard_map/pad | solution.py:78
  348.1 4.3 add.255
  355.3 5.0 fusion.16
  362.0 18.6 %pad.96 = f32[64,16,1024]{2,1,0:T(8,128)} pad(f32[32,16,1024]{2,1,0:T(8,128)} %pad_maximum_fusion.2, f32[]{:T(128)} %constant.13.clone.1), padding=0_1_1x0_0_0x0_0_0 | pad | bytes 6291460 | tf_op jit(solution)/shard_map/pad | solution.py:78
  380.6 12.0 %pad.97 = f32[64,16,1024]{2,1,0:T(8,128)} pad(f32[32,16,1024]{2,1,0:T(8,128)S(1)} %copy-done.16, f32[]{:T(128)} %constant.13.clone.1), padding=1_0_1x0_0_0x0_0_0 | pad | bytes 6291460 | tf_op jit(solution)/shard_map/pad | solution.py:78
  392.5 6.8 add.257
  399.4 35.6 %pad.99 = f32[128,16,1024]{2,1,0:T(8,128)} pad(f32[64,16,1024]{2,1,0:T(8,128)} %add.257, f32[]{:T(128)} %constant.13.clone.1), padding=1_0_1x0_0_0x0_0_0 | pad | bytes 12582916 | tf_op jit(solution)/shard_map/pad | solution.py:78
  436.5 18.6 %pad.110 = f32[64,16,1024]{2,1,0:T(8,128)} pad(f32[32,16,1024]{2,1,0:T(8,128)} %pad_maximum_fusion.3, f32[]{:T(128)} %constant.13.clone.1), padding=0_1_1x0_0_0x0_0_0 | pad | bytes 6291460 | tf_op jit(solution)/shard_map/pad | solution.py:78
  455.1 11.9 %pad.111 = f32[64,16,1024]{2,1,0:T(8,128)} pad(f32[32,16,1024]{2,1,0:T(8,128)S(1)} %copy-done.15, f32[]{:T(128)} %constant.13.clone.1), padding=1_0_1x0_0_0x0_0_0 | pad | bytes 6291460 | tf_op jit(solution)/shard_map/pad | solution.py:78
  467.0 7.1 add.265
  475.6 7.6 fusion.12
  483.2 2.5 pad_maximum_fusion
  485.7 35.5 %pad.98 = f32[128,16,1024]{2,1,0:T(8,128)} pad(f32[64,16,1024]{2,1,0:T(8,128)} %pad_maximum_fusion, f32[]{:T(128)} %constant.13.clone.1), padding=0_1_1x0_0_0x0_0_0 | pad | bytes 12582916 | tf_op jit(solution)/shard_map/pad | solution.py:78
  521.2 35.5 %pad.113 = f32[128,16,1024]{2,1,0:T(8,128)} pad(f32[64,16,1024]{2,1,0:T(8,128)} %add.265, f32[]{:T(128)} %constant.13.clone.1), padding=1_0_1x0_0_0x0_0_0 | pad | bytes 12582916 | tf_op jit(solution)/shard_map/pad | solution.py:78
  556.8 4.8 pad_maximum_fusion.1
  561.5 35.5 %pad.112 = f32[128,16,1024]{2,1,0:T(8,128)} pad(f32[64,16,1024]{2,1,0:T(8,128)} %pad_maximum_fusion.1, f32[]{:T(128)} %constant.13.clone.1), padding=0_1_1x0_0_0x0_0_0 | pad | bytes 12582916 | tf_op jit(solution)/shard_map/pad | solution.py:78
  598.8 107.7 %while.11 = (s32[]{:T(128)}, f32[16,1024]{1,0:T(8,128)S(1)}, f32[16,1024]{1,0:T(8,128)S(1)}, f32[16,1024]{1,0:T(8,128)S(1)}, s32[]{:T(128)}, /*index=5*/s32[]{:T(128)}) while((s32[]{:T(128)}, f32[16,1024]{1,0:T(8,128)S(1)}, f32[16,1024]{1,0:T(8,128)S(1)}, f32[16,1024]{1,0:T(8,128)S(1)}, s32[]{:T(128)}, /*index=5*/s32[]{:T(128)}) %tuple.47), condition=%wide.region_4.5_spmd.clone, body=%wide.region_3.4_spmd.clone.sunk | while | flops 81923 | bytes 458871 | solution.py:87
  598.8 3.4 collective-permute-start
  603.9 4.2 collective-permute-start
  609.7 4.3 collective-permute-start
  615.6 4.2 collective-permute-start
  621.5 4.2 collective-permute-start
  627.3 5.6 collective-permute-start
  634.5 6.5 collective-permute-start
  642.6 6.5 collective-permute-start
  650.7 6.3 collective-permute-start
  658.6 6.3 collective-permute-start
  666.6 6.3 collective-permute-start
  674.6 6.2 collective-permute-start
  682.5 6.3 collective-permute-start
  690.4 6.5 collective-permute-start
  698.5 6.3 collective-permute-start
  706.5 14.0 %multiply_reduce_fusion = f32[128,1024]{1,0:T(8,128)S(1)} fusion(f32[128,16,1024]{2,1,0:T(8,128)} %pad.112, f32[128,16,1024]{2,1,0:T(8,128)} %pad.113, f32[128,16,1024]{2,1,0:T(8,128)} %pad.98, f32[128,16,1024]{2,1,0:T(8,128)} %pad.99, f32[16,1024]{1,0:T(8,128)S(1)} %get-tuple-element.27, f32[128,16]{1,0:T(8,128)S(1)} %copy-done.28), kind=kLoop, calls=%fused_computation.3 | loop fusion | flops 12451840 | bytes 34152448 | tf_op jit(solution)/shard_map/reduce_sum | solution.py:89
  720.5 5.7 convolution_convert_fusion
  727.1 39.7 %reduce-scatter.3.cloned.1.call-done = bf16[16,4096]{1,0:T(8,128)(2,1)} async-done(((bf16[128,4096]{1,0:T(8,128)(2,1)}), bf16[16,4096]{1,0:T(8,128)(2,1)}) %reduce-scatter.3.cloned.1.call-update) | async-done | bytes 131088 | tf_op jit(solution)/shard_map/reduce_scatter | solution.py:96
  769.3 16.9 %all_to_all.10 = bf16[16,4,4096]{2,1,0:T(4,128)(2,1)S(1)} all-to-all(bf16[16,4,4096]{2,1,0:T(4,128)(2,1)S(1)} %reshape.78), channel_id=1, replica_groups=mesh['seq'=16,'expert'=8] {'seq'}, dimensions={0} | all-to-all | bytes 1048576 | tf_op jit(solution)/shard_map/all_to_all | solution.py:113
  787.2 29.3 %all-gather.11.cloned.1.call-done = bf16[8,64,4096]{2,1,0:T(8,128)(2,1)} async-done(((bf16[1,64,4096]{2,1,0:T(8,128)(2,1)}), bf16[8,64,4096]{2,1,0:T(8,128)(2,1)}) %all-gather.11.cloned.1.call-update) | async-done | bytes 4194320 | tf_op jit(solution)/shard_map/all_gather | solution.py:116
  816.5 10.1 %fusion.6 = f32[512,896]{1,0:T(8,128)} fusion(bf16[512,4096]{1,0:T(8,128)(2,1)} %bitcast.51, bf16[1,4096,896]{2,1,0:T(8,128)(2,1)} %param.33), kind=kOutput, calls=%fused_computation.9 | convolution fusion | flops 3758096384 | bytes 13369344 | tf_op jit(solution)/shard_map/dot_general | solution.py:119
  826.6 16.7 %fusion.8 = bf16[512,4096]{1,0:T(8,128)(2,1)} fusion(bf16[1,896,4096]{2,1,0:T(8,128)(2,1)} %param.35, f32[512,896]{1,0:T(8,128)} %fusion.6, bf16[512,4096]{1,0:T(8,128)(2,1)} %bitcast.52, bf16[1,4096,896]{2,1,0:T(8,128)(2,1)} %param.34), kind=kOutput, calls=%fused_computation.11 | convolution fusion | flops 7521042432 | bytes 24903680 | tf_op jit(solution)/shard_map/dot_general | solution.py:123
  843.3 38.0 %reduce-scatter.5.cloned.1.call-done = bf16[64,4096]{1,0:T(8,128)(2,1)} async-done(((bf16[512,4096]{1,0:T(8,128)(2,1)}), bf16[64,4096]{1,0:T(8,128)(2,1)}) %reduce-scatter.5.cloned.1.call-update) | async-done | bytes 524304 | tf_op jit(solution)/shard_map/reduce_scatter | solution.py:122
  883.3 7.1 all-to-all-start.1
  890.5 10.1 %all-to-all-done.1 = bf16[16,4,4096]{2,1,0:T(4,128)(2,1)S(1)} async-done(((bf16[16,4,4096]{2,1,0:T(4,128)(2,1)}), bf16[16,4,4096]{2,1,0:T(4,128)(2,1)S(1)}, u32[]{:S(2)}, u32[]{:S(2)}) %all-to-all-start.1) | async-done | bytes 524320 | tf_op jit(solution)/shard_map/all_to_all | solution.py:128
  (225 shorter events, 89.7 us)
Async XLA Ops:
  6.5 155.7 %copy-start = (bf16[1024,288]{0,1:T(8,128)(2,1)S(1)}, bf16[1024,288]{0,1:T(8,128)(2,1)}, u32[]{:S(2)}) copy-start(bf16[1024,288]{0,1:T(8,128)(2,1)} %param.24) | copy-start | bytes 1769476
  6.5 28.4 %all-gather.5.cloned.1.call-start = ((), (), s32[]{:S(2)}) async-start(), calls=%async_computation.4 | async-start | bytes 1179648 | tf_op jit(solution)/shard_map/all_gather | solution.py:49
  7.3 141.1 %all-gather.7.cloned.1.call-start = ((), (), s32[]{:S(2)}) async-start(), calls=%async_computation.5 | async-start | bytes 17825792 | tf_op jit(solution)/shard_map/all_gather | solution.py:55
  8.0 215.6 %all-reduce.30.cloned.1.call-start = ((), (), s32[]{:S(2)}) async-start(), calls=%async_computation.6 | async-start | bytes 131072 | tf_op jit(solution)/shard_map/psum | solution.py:68
  36.4 125.5 %copy-start.39 = (f32[1024]{0:T(1024)S(1)}, f32[1024]{0:T(1024)}, u32[]{:S(2)}) copy-start(f32[1024]{0:T(1024)} %param.23) | copy-start | bytes 12292
  36.4 187.1 %copy-start.42 = (bf16[256,1024]{1,0:T(8,128)(2,1)S(1)}, bf16[256,1024]{1,0:T(8,128)(2,1)}, u32[]{:S(2)}) copy-start(bf16[256,1024]{1,0:T(8,128)(2,1)} %param.25) | copy-start | bytes 1572868
  36.4 187.1 %copy-start.43 = (f32[1024]{0:T(1024)S(1)}, f32[1024]{0:T(1024)}, u32[]{:S(2)}) copy-start(f32[1024]{0:T(1024)} %param.26) | copy-start | bytes 12292
  156.9 3.6 copy-start.18
  156.9 68.0 %copy-start.37 = (f32[16,1024]{1,0:T(8,128)S(1)}, f32[16,1024]{1,0:T(8,128)}, u32[]{:S(2)}) copy-start(f32[16,1024]{1,0:T(8,128)} %param.27) | copy-start | bytes 196612
  156.9 5.0 collective-permute-start.1
  162.2 64.8 %copy-start.23 = (bf16[128,1024]{1,0:T(8,128)(2,1)}, bf16[128,1024]{1,0:T(8,128)(2,1)S(1)}, u32[]{:S(2)}) copy-start(bf16[128,1024]{1,0:T(8,128)(2,1)S(1)} %multiply_convert_fusion.1) | copy-start | bytes 786436
  163.2 557.3 %all-gather.9.cloned.1.call-start = ((), (), s32[]{:S(2)}) async-start(), calls=%async_computation.7 | async-start | bytes 8912896 | tf_op jit(solution)/shard_map/all_gather | solution.py:93
  163.8 602.9 %reduce-scatter.3.cloned.1.call-start = ((), (), s32[]{:S(2)}) async-start(), calls=%async_computation.8 | async-start | bytes 1179648 | tf_op jit(solution)/shard_map/reduce_scatter | solution.py:96
  227.0 3.3 copy-start.3
  227.0 5.8 copy-start.2
  244.4 5.5 copy-start.7
  249.9 3.8 copy-start.11
  249.9 3.8 copy-start.12
  280.3 8.2 copy-start.36
  286.3 5.9 copy-start.35
  288.5 8.3 copy-start.20
  300.3 3.8 copy-start.13
  300.3 3.8 copy-start.14
  304.1 3.1 copy-start.34
  308.4 27.3 %copy-start.33 = (f32[1,16,1024]{2,1,0:T(8,128)S(1)}, f32[1,16,1024]{2,1,0:T(8,128)}, u32[]{:S(2)}) copy-start(f32[1,16,1024]{2,1,0:T(8,128)} %slice.347) | copy-start | bytes 196612
  348.1 4.3 copy-start.8
  355.3 5.0 copy-start.32
  362.0 18.6 %copy-start.16 = (f32[32,16,1024]{2,1,0:T(8,128)S(1)}, f32[32,16,1024]{2,1,0:T(8,128)}, u32[]{:S(2)}) copy-start(f32[32,16,1024]{2,1,0:T(8,128)} %add.255) | copy-start | bytes 6291460
  399.4 35.6 %copy-start.17 = (f32[31,16,1024]{2,1,0:T(8,128)S(1)}, f32[31,16,1024]{2,1,0:T(8,128)}, u32[]{:S(2)}) copy-start(f32[31,16,1024]{2,1,0:T(8,128)} %get-tuple-element.56) | copy-start | bytes 6094852
  399.4 35.6 %copy-start.31 = (f32[1,16,1024]{2,1,0:T(8,128)S(1)}, f32[1,16,1024]{2,1,0:T(8,128)}, u32[]{:S(2)}) copy-start(f32[1,16,1024]{2,1,0:T(8,128)} %slice.369) | copy-start | bytes 196612
  436.5 18.6 %copy-start.15 = (f32[32,16,1024]{2,1,0:T(8,128)S(1)}, f32[32,16,1024]{2,1,0:T(8,128)}, u32[]{:S(2)}) copy-start(f32[32,16,1024]{2,1,0:T(8,128)} %add.264) | copy-start | bytes 6291460
  467.0 7.1 copy-start.4
  467.0 7.1 copy-start.5
  467.0 8.6 copy-start.6
  475.6 7.6 copy-start.30
  521.2 35.5 %copy-start.29 = (f32[1,16,1024]{2,1,0:T(8,128)S(1)}, f32[1,16,1024]{2,1,0:T(8,128)}, u32[]{:S(2)}) copy-start(f32[1,16,1024]{2,1,0:T(8,128)} %slice.368) | copy-start | bytes 196612
  561.5 144.9 %copy-start.28 = (f32[128,16]{1,0:T(8,128)S(1)}, f32[128,16]{1,0:T(8,128)}, u32[]{:S(2)}) copy-start(f32[128,16]{1,0:T(8,128)} %copy.42) | copy-start | bytes 24580
  598.8 5.0 collective-permute-start
  603.9 5.8 collective-permute-start
  609.7 5.9 collective-permute-start
  615.6 5.8 collective-permute-start
  621.5 5.8 collective-permute-start
  627.3 7.2 collective-permute-start
  634.5 8.1 collective-permute-start
  642.6 8.1 collective-permute-start
  650.7 7.9 collective-permute-start
  658.6 7.9 collective-permute-start
  666.6 8.0 collective-permute-start
  674.6 7.8 collective-permute-start
  682.5 7.9 collective-permute-start
  690.4 8.1 collective-permute-start
  698.5 7.9 collective-permute-start
  706.5 14.1 %copy-start.19 = (f32[128,2,1024]{2,0,1:T(8,128)S(1)}, f32[128,2,1024]{2,0,1:T(8,128)}, u32[]{:S(2)}) copy-start(f32[128,2,1024]{2,0,1:T(8,128)} %copy-done.18) | copy-start | bytes 3145732
  706.5 14.1 %copy-start.24 = (bf16[128,1024]{1,0:T(8,128)(2,1)S(1)}, bf16[128,1024]{1,0:T(8,128)(2,1)}, u32[]{:S(2)}) copy-start(bf16[128,1024]{1,0:T(8,128)(2,1)} %copy-done.23) | copy-start | bytes 786436
  706.5 14.1 %copy-start.44 = (f32[1024]{0:T(1024)S(1)}, f32[1024]{0:T(1024)}, u32[]{:S(2)}) copy-start(f32[1024]{0:T(1024)} %param.28) | copy-start | bytes 12292
  720.5 5.9 copy-start.40
  720.5 46.3 %copy-start.21 = (bf16[16,4096]{1,0:T(8,128)(2,1)S(1)}, bf16[16,4096]{1,0:T(8,128)(2,1)}, u32[]{:S(2)}) copy-start(bf16[16,4096]{1,0:T(8,128)(2,1)} %param.19) | copy-start | bytes 393220
  720.5 47.3 %copy-start.38 = (f32[4096]{0:T(1024)S(1)}, f32[4096]{0:T(1024)}, u32[]{:S(2)}) copy-start(f32[4096]{0:T(1024)} %param.30) | copy-start | bytes 49156
  726.3 90.2 %all-gather.11.cloned.1.call-start = ((), (), s32[]{:S(2)}) async-start(), calls=%async_computation.9 | async-start | bytes 4718592 | tf_op jit(solution)/shard_map/all_gather | solution.py:116
  787.1 94.2 %reduce-scatter.5.cloned.1.call-start = ((), (), s32[]{:S(2)}) async-start(), calls=%async_computation.10 | async-start | bytes 4718592 | tf_op jit(solution)/shard_map/reduce_scatter | solution.py:122
  826.6 75.1 %copy-start.1 = (bf16[1024,288]{0,1:T(8,128)(2,1)S(1)}, bf16[1024,288]{0,1:T(8,128)(2,1)}, u32[]{:S(2)}) copy-start(bf16[1024,288]{0,1:T(8,128)(2,1)} %param.24) | copy-start | bytes 1769476
  843.2 47.2 %copy-start.41 = (f32[16,2]{0,1:T(2,128)S(1)}, f32[16,2]{0,1:T(2,128)}, u32[]{:S(2)}) copy-start(f32[16,2]{0,1:T(2,128)} %param.32) | copy-start | bytes 388
  843.2 57.4 %copy-start.22 = (bf16[16,4096]{1,0:T(8,128)(2,1)S(1)}, bf16[16,4096]{1,0:T(8,128)(2,1)}, u32[]{:S(2)}) copy-start(bf16[16,4096]{1,0:T(8,128)(2,1)} %reduce-scatter.3.cloned.1.call-done) | copy-start | bytes 393220
  883.3 17.2 %all-to-all-start.1 = ((bf16[16,4,4096]{2,1,0:T(4,128)(2,1)}), bf16[16,4,4096]{2,1,0:T(4,128)(2,1)S(1)}, u32[]{:S(2)}, u32[]{:S(2)}) async-start(bf16[16,4,4096]{2,1,0:T(4,128)(2,1)} %reshape.81), calls=%async_computation.3 | async-start | bytes 1048576 | tf_op jit(solution)/shard_map/all_to_all | solution.py:128
  (5 other events, 7.3 us)
Sparse Core Ops, SparseCore 0:
  9.1 25.7 all-gather.4
  37.0 111.3 all-gather.6
  163.4 60.1 all-reduce.29
  225.7 77.5 all-gather.8
  726.4 40.3 reduce-scatter.2
  787.2 29.2 all-gather.10
  843.4 37.8 reduce-scatter.4
where the time goes:
time: 924 us; the launch traced here: 909 us
  waiting for transfers between devices  327 us (35%)
  local copies, waits for them, and re-layouts  289 us (31%)
  other arithmetic  109 us (12%)
  starting transfers between devices  94.2 us (10%)
  matrix products  44.8 us (5%)
  blocking collectives  30.9 us (3%)
  between operations  14 us (2%)
    pad x24, local copies, waits for them, and re-layouts, per_device(): lax.associative_scan(combine_states, (decay, source), axis=0)  267 us
    all_gather x1, waiting for transfers between devices, per_device(): lax.all_gather(in_weight, 'seq', axis=1, tiled=True)  112 us
    ppermute x16, starting transfers between devices, from_behind(): return lax.ppermute(block, axis, route)  86.9 us
    psum x1, waiting for transfers between devices, per_device(): lax.psum(partial_value[:, :RANK].astype(jnp.bfloat16), 'expert')  44.8 us
    reduce_scatter x1, waiting for transfers between devices, per_device(): lax.psum_scatter(terms.astype(jnp.bfloat16), 'expert', scatter_dimension=...  39.7 us
    reduce_scatter x1, waiting for transfers between devices, per_device(): lax.psum_scatter(jnp.dot(act, w_down[0], preferred_element_type=jnp.float...  38 us
    add x12, other arithmetic, combine_states(): return (earlier[0] * later[0], later[0] * earlier[1] + later[1])  34.6 us
    add x12, other arithmetic, per_device(): lax.associative_scan(combine_states, (decay, source), axis=0)  33.2 us
  transfers between devices with their start and end apart: 24, of which 23 were waited for; matrix products, arithmetic and copies ran while one was open for 42% of the time, Pallas kernels for 0%

commit v1 on v0

--- a/solution.py
+++ b/solution.py
@@ -7,6 +7,21 @@
 CONV = 4
 RANK = 256
 TOP = 2
+
+
+def state_routes_all_for(vec, axis_tag, at_axis):
+    world_n = lax.axis_size(axis_tag)
+    all_blocks = [(w, (w + 1) % world_n) for w in range(world_n)]
+    parts_out = [None] * world_n
+    parts_out[world_n - 1] = vec
+    for j0 in range(world_n - 2, -1, -1):
+        parts_out[j0] = lax.ppermute(parts_out[j0 + 1], axis_name=axis_tag, perm=all_blocks)
+    low = jnp.roll(
+        jnp.concatenate(parts_out, at_axis),
+        (lax.axis_index(axis_tag) + 1) * vec.shape[at_axis],
+        at_axis,
+    )
+    return low
 
 
 def from_behind(block, axis, distance):
@@ -46,7 +61,7 @@
     rows, dim = tokens.shape
     n_seq = lax.axis_size("seq")
     n_exp = lax.axis_size("expert")
-    group = lax.all_gather(tokens, "expert", axis=0, tiled=True)
+    group = state_routes_all_for(tokens, "expert", 0)
     local_tok = group.shape[0]
     normed = rms_norm(group, gain_mamba).astype(jnp.bfloat16)
     both = jnp.einsum(

time: 924 us -> 896 us (0.970)
  waiting for transfers between devices: 327 us -> 302 us
    ppermute x0 -> x7, waiting for transfers between devices: none -> 38.5 us  [state_routes_all_for(): lax.ppermute(parts_out[j0 + 1], axis_name=axis_tag, perm=all_blocks)]
    all_gather x1, waiting for transfers between devices: 112 us -> 75.1 us  [per_device(): lax.all_gather(in_weight, 'seq', axis=1, tiled=True)]
    all_gather x1 -> x0, waiting for transfers between devices: 26 us -> none  [per_device(): group = lax.all_gather(tokens, 'expert', axis=0, tiled=True)]
  transfers between devices with their start and end apart: 24 -> 30, of which waited for: 23 -> 29; matrix products, arithmetic and copies ran while one was open for 42% -> 43% of each run, Pallas kernels for 0% -> 0%
where the time goes in v1:
time: 896 us; the launch traced here: 881 us
  waiting for transfers between devices  302 us (34%)
  local copies, waits for them, and re-layouts  291 us (32%)
  other arithmetic  104 us (12%)
  starting transfers between devices  94.3 us (11%)
  matrix products  44.4 us (5%)
  blocking collectives  30.9 us (3%)
  between operations  14.2 us (2%)
    pad x24, local copies, waits for them, and re-layouts, per_device(): lax.associative_scan(combine_states, (decay, source), axis=0)  266 us
    ppermute x16, starting transfers between devices, from_behind(): return lax.ppermute(block, axis, route)  87 us
    all_gather x1, waiting for transfers between devices, per_device(): lax.all_gather(in_weight, 'seq', axis=1, tiled=True)  75.1 us
    psum x1, waiting for transfers between devices, per_device(): lax.psum(partial_value[:, :RANK].astype(jnp.bfloat16), 'expert')  44.7 us
    reduce_scatter x1, waiting for transfers between devices, per_device(): lax.psum_scatter(terms.astype(jnp.bfloat16), 'expert', scatter_dimension=...  39.7 us
    ppermute x7, waiting for transfers between devices, state_routes_all_for(): lax.ppermute(parts_out[j0 + 1], axis_name=axis_tag, perm=all_blocks)  38.5 us
    reduce_scatter x1, waiting for transfers between devices, per_device(): lax.psum_scatter(jnp.dot(act, w_down[0], preferred_element_type=jnp.float...  38 us
    add x12, other arithmetic, combine_states(): return (earlier[0] * later[0], later[0] * earlier[1] + later[1])  32.8 us
  transfers between devices with their start and end apart: 30, of which 29 were waited for; matrix products, arithmetic and copies ran while one was open for 43% of the time, Pallas kernels for 0%

profile of v1, /device:TPU:0, one launch (start us, length us, event | category | flops | bytes accessed | tf_op | source)
XLA Modules:
  0.0 880.8 jit_solution(14474350114319503244)
XLA Ops:
  7.3 5.8 collective-permute-done.1
  13.1 5.6 collective-permute-done.2
  18.7 5.6 collective-permute-done.3
  24.3 5.6 collective-permute-done.4
  29.9 5.6 collective-permute-done.5
  35.6 5.6 collective-permute-done.6
  42.1 4.7 collective-permute-done.7
  48.4 75.1 %all-gather.4.cloned.1.call-done = bf16[2,4096,1024]{2,1,0:T(8,128)(2,1)} async-done(((bf16[2,256,1024]{2,1,0:T(8,128)(2,1)}), bf16[2,4096,1024]{2,1,0:T(8,128)(2,1)}) %all-gather.4.cloned.1.call-update) | async-done | bytes 16777232 | tf_op jit(solution)/shard_map/all_gather | solution.py:70
  123.4 8.1 fusion.20
  131.6 3.5 collective-permute-start.8
  138.8 14.0 %psum.14 = bf16[128,32]{0,1:T(8,128)(2,1)S(1)} all-reduce(bf16[128,32]{0,1:T(8,128)(2,1)S(1)} %slice.341), channel_id=1, replica_groups=mesh['seq'=16,'expert'=8] {'expert'}, use_global_device_ids=true, to_apply=%region_1.2 | all-reduce | flops 4096 | bytes 16384 | tf_op jit(solution)/shard_map/psum | solution.py:84
  153.6 44.7 %all-reduce.30.cloned.1.call-done = bf16[128,256]{0,1:T(8,128)(2,1)} async-done(((bf16[128,256]{0,1:T(8,128)(2,1)}), bf16[128,256]{0,1:T(8,128)(2,1)}) %all-reduce.30.cloned.1.call-update) | async-done | bytes 65552 | tf_op jit(solution)/shard_map/psum | solution.py:83
  201.7 3.3 copy-done.3
  208.2 10.9 %slice_add_fusion = (f32[64,16,1024]{2,1,0:T(8,128)S(1)}, f32[64,16,1024]{2,1,0:T(8,128)}) fusion(f32[128,16,1024]{2,1,0:T(8,128)} %copy-done.3, f32[128,16,1024]{2,1,0:T(8,128)} %copy-done.2), kind=kLoop, calls=%fused_computation.19 | loop fusion | flops 3145728 | bytes 25165824 | tf_op jit(solution)/shard_map/add | solution.py:39
  221.4 3.3 slice_add_fusion.1
  251.1 3.7 pad.91
  256.4 3.8 pad.90
  266.4 3.5 pad.92
  269.9 3.5 pad.93
  276.5 3.1 fusion.24
  280.7 7.0 pad.108
  287.7 10.2 %pad.109 = f32[32,16,1024]{2,1,0:T(8,128)} pad(f32[16,16,1024]{2,1,0:T(8,128)} %add.279, f32[]{:T(128)} %constant.56.clone.1), padding=1_0_1x0_0_0x0_0_0 | pad | bytes 3145732 | tf_op jit(solution)/shard_map/pad | solution.py:93
  297.9 10.1 %pad.95 = f32[32,16,1024]{2,1,0:T(8,128)} pad(f32[16,16,1024]{2,1,0:T(8,128)} %add.269, f32[]{:T(128)} %constant.56.clone.1), padding=1_0_1x0_0_0x0_0_0 | pad | bytes 3145732 | tf_op jit(solution)/shard_map/pad | solution.py:93
  310.2 10.1 %pad.94 = f32[32,16,1024]{2,1,0:T(8,128)} pad(f32[16,16,1024]{2,1,0:T(8,128)} %pad_maximum_fusion.4, f32[]{:T(128)} %constant.56.clone.1), padding=0_1_1x0_0_0x0_0_0 | pad | bytes 3145732 | tf_op jit(solution)/shard_map/pad | solution.py:93
  320.4 4.2 add.271
  327.6 5.0 fusion.16
  334.2 18.6 %pad.96 = f32[64,16,1024]{2,1,0:T(8,128)} pad(f32[32,16,1024]{2,1,0:T(8,128)} %pad_maximum_fusion.2, f32[]{:T(128)} %constant.56.clone.1), padding=0_1_1x0_0_0x0_0_0 | pad | bytes 6291460 | tf_op jit(solution)/shard_map/pad | solution.py:93
  352.8 11.9 %pad.97 = f32[64,16,1024]{2,1,0:T(8,128)} pad(f32[32,16,1024]{2,1,0:T(8,128)S(1)} %copy-done.16, f32[]{:T(128)} %constant.56.clone.1), padding=1_0_1x0_0_0x0_0_0 | pad | bytes 6291460 | tf_op jit(solution)/shard_map/pad | solution.py:93
  364.7 6.9 add.273
  371.6 35.6 %pad.99 = f32[128,16,1024]{2,1,0:T(8,128)} pad(f32[64,16,1024]{2,1,0:T(8,128)} %add.273, f32[]{:T(128)} %constant.56.clone.1), padding=1_0_1x0_0_0x0_0_0 | pad | bytes 12582916 | tf_op jit(solution)/shard_map/pad | solution.py:93
  408.7 18.6 %pad.110 = f32[64,16,1024]{2,1,0:T(8,128)} pad(f32[32,16,1024]{2,1,0:T(8,128)} %pad_maximum_fusion.3, f32[]{:T(128)} %constant.56.clone.1), padding=0_1_1x0_0_0x0_0_0 | pad | bytes 6291460 | tf_op jit(solution)/shard_map/pad | solution.py:93
  427.2 11.9 %pad.111 = f32[64,16,1024]{2,1,0:T(8,128)} pad(f32[32,16,1024]{2,1,0:T(8,128)S(1)} %copy-done.15, f32[]{:T(128)} %constant.56.clone.1), padding=1_0_1x0_0_0x0_0_0 | pad | bytes 6291460 | tf_op jit(solution)/shard_map/pad | solution.py:93
  439.2 7.1 add.281
  447.8 7.5 fusion.12
  457.9 35.5 %pad.98 = f32[128,16,1024]{2,1,0:T(8,128)} pad(f32[64,16,1024]{2,1,0:T(8,128)} %pad_maximum_fusion, f32[]{:T(128)} %constant.56.clone.1), padding=0_1_1x0_0_0x0_0_0 | pad | bytes 12582916 | tf_op jit(solution)/shard_map/pad | solution.py:93
  493.4 35.5 %pad.113 = f32[128,16,1024]{2,1,0:T(8,128)} pad(f32[64,16,1024]{2,1,0:T(8,128)} %add.281, f32[]{:T(128)} %constant.56.clone.1), padding=1_0_1x0_0_0x0_0_0 | pad | bytes 12582916 | tf_op jit(solution)/shard_map/pad | solution.py:93
  529.0 4.8 pad_maximum_fusion.1
  533.8 35.5 %pad.112 = f32[128,16,1024]{2,1,0:T(8,128)} pad(f32[64,16,1024]{2,1,0:T(8,128)} %pad_maximum_fusion.1, f32[]{:T(128)} %constant.56.clone.1), padding=0_1_1x0_0_0x0_0_0 | pad | bytes 12582916 | tf_op jit(solution)/shard_map/pad | solution.py:93
  571.1 107.7 %while.11 = (s32[]{:T(128)}, f32[16,1024]{1,0:T(8,128)S(1)}, f32[16,1024]{1,0:T(8,128)S(1)}, f32[16,1024]{1,0:T(8,128)S(1)}, s32[]{:T(128)}, /*index=5*/s32[]{:T(128)}) while((s32[]{:T(128)}, f32[16,1024]{1,0:T(8,128)S(1)}, f32[16,1024]{1,0:T(8,128)S(1)}, f32[16,1024]{1,0:T(8,128)S(1)}, s32[]{:T(128)}, /*index=5*/s32[]{:T(128)}) %tuple.47), condition=%wide.region_4.5_spmd.clone, body=%wide.region_3.4_spmd.clone.sunk | while | flops 81923 | bytes 458871 | solution.py:102
  571.1 3.4 collective-permute-start
  576.2 4.2 collective-permute-start
  582.0 4.4 collective-permute-start
  588.0 4.2 collective-permute-start
  593.8 4.2 collective-permute-start
  599.7 5.5 collective-permute-start
  606.8 6.5 collective-permute-start
  614.9 6.5 collective-permute-start
  623.0 6.3 collective-permute-start
  630.9 6.3 collective-permute-start
  638.9 6.3 collective-permute-start
  646.9 6.3 collective-permute-start
  654.8 6.4 collective-permute-start
  662.7 6.5 collective-permute-start
  670.9 6.3 collective-permute-start
  678.8 14.0 %multiply_reduce_fusion = f32[128,1024]{1,0:T(8,128)S(1)} fusion(f32[128,16,1024]{2,1,0:T(8,128)} %pad.112, f32[128,16,1024]{2,1,0:T(8,128)} %pad.113, f32[128,16,1024]{2,1,0:T(8,128)} %pad.98, f32[128,16,1024]{2,1,0:T(8,128)} %pad.99, f32[16,1024]{1,0:T(8,128)S(1)} %get-tuple-element.27, f32[128,16]{1,0:T(8,128)S(1)} %copy-done.31), kind=kLoop, calls=%fused_computation.3 | loop fusion | flops 12451840 | bytes 34152448 | tf_op jit(solution)/shard_map/reduce_sum | solution.py:104
  692.9 5.7 convolution_convert_fusion
  699.4 39.7 %reduce-scatter.3.cloned.1.call-done = bf16[16,4096]{1,0:T(8,128)(2,1)} async-done(((bf16[128,4096]{1,0:T(8,128)(2,1)}), bf16[16,4096]{1,0:T(8,128)(2,1)}) %reduce-scatter.3.cloned.1.call-update) | async-done | bytes 131088 | tf_op jit(solution)/shard_map/reduce_scatter | solution.py:111
  741.6 16.9 %all_to_all.10 = bf16[16,4,4096]{2,1,0:T(4,128)(2,1)S(1)} all-to-all(bf16[16,4,4096]{2,1,0:T(4,128)(2,1)S(1)} %reshape.78), channel_id=1, replica_groups=mesh['seq'=16,'expert'=8] {'seq'}, dimensions={0} | all-to-all | bytes 1048576 | tf_op jit(solution)/shard_map/all_to_all | solution.py:128
  759.6 29.3 %all-gather.8.cloned.1.call-done = bf16[8,64,4096]{2,1,0:T(8,128)(2,1)} async-done(((bf16[1,64,4096]{2,1,0:T(8,128)(2,1)}), bf16[8,64,4096]{2,1,0:T(8,128)(2,1)}) %all-gather.8.cloned.1.call-update) | async-done | bytes 4194320 | tf_op jit(solution)/shard_map/all_gather | solution.py:131
  788.9 10.1 %fusion.6 = f32[512,896]{1,0:T(8,128)} fusion(bf16[512,4096]{1,0:T(8,128)(2,1)} %bitcast.51, bf16[1,4096,896]{2,1,0:T(8,128)(2,1)} %param.33), kind=kOutput, calls=%fused_computation.9 | convolution fusion | flops 3758096384 | bytes 13369344 | tf_op jit(solution)/shard_map/dot_general | solution.py:134
  798.9 16.6 %fusion.8 = bf16[512,4096]{1,0:T(8,128)(2,1)} fusion(bf16[1,896,4096]{2,1,0:T(8,128)(2,1)} %param.35, f32[512,896]{1,0:T(8,128)} %fusion.6, bf16[512,4096]{1,0:T(8,128)(2,1)} %bitcast.52, bf16[1,4096,896]{2,1,0:T(8,128)(2,1)} %param.34), kind=kOutput, calls=%fused_computation.11 | convolution fusion | flops 7521042432 | bytes 24903680 | tf_op jit(solution)/shard_map/dot_general | solution.py:138
  815.6 38.0 %reduce-scatter.5.cloned.1.call-done = bf16[64,4096]{1,0:T(8,128)(2,1)} async-done(((bf16[512,4096]{1,0:T(8,128)(2,1)}), bf16[64,4096]{1,0:T(8,128)(2,1)}) %reduce-scatter.5.cloned.1.call-update) | async-done | bytes 524304 | tf_op jit(solution)/shard_map/reduce_scatter | solution.py:137
  855.7 7.1 all-to-all-start.1
  862.8 10.1 %all-to-all-done.1 = bf16[16,4,4096]{2,1,0:T(4,128)(2,1)S(1)} async-done(((bf16[16,4,4096]{2,1,0:T(4,128)(2,1)}), bf16[16,4,4096]{2,1,0:T(4,128)(2,1)S(1)}, u32[]{:S(2)}, u32[]{:S(2)}) %all-to-all-start.1) | async-done | bytes 524320 | tf_op jit(solution)/shard_map/all_to_all | solution.py:143
  (260 shorter events, 100.5 us)
Async XLA Ops:
  6.5 130.4 %copy-start = (bf16[1024,288]{0,1:T(8,128)(2,1)S(1)}, bf16[1024,288]{0,1:T(8,128)(2,1)}, u32[]{:S(2)}) copy-start(bf16[1024,288]{0,1:T(8,128)(2,1)} %param.24) | copy-start | bytes 1769476
  6.5 41.3 %copy-start.22 = (bf16[16,4096]{1,0:T(8,128)(2,1)S(1)}, bf16[16,4096]{1,0:T(8,128)(2,1)}, u32[]{:S(2)}) copy-start(bf16[16,4096]{1,0:T(8,128)(2,1)} %param.19) | copy-start | bytes 393220
  6.5 116.9 %all-gather.4.cloned.1.call-start = ((), (), s32[]{:S(2)}) async-start(), calls=%async_computation.4 | async-start | bytes 17825792 | tf_op jit(solution)/shard_map/all_gather | solution.py:70
  7.3 191.0 %all-reduce.30.cloned.1.call-start = ((), (), s32[]{:S(2)}) async-start(), calls=%async_computation.5 | async-start | bytes 131072 | tf_op jit(solution)/shard_map/psum | solution.py:83
  7.3 5.8 collective-permute-start.1
  13.1 5.6 collective-permute-start.2
  18.7 5.6 collective-permute-start.3
  24.3 5.6 collective-permute-start.4
  29.9 5.6 collective-permute-start.5
  35.5 5.6 collective-permute-start.6
  41.2 5.6 collective-permute-start.7
  47.8 75.7 %copy-start.41 = (f32[4096]{0:T(1024)S(1)}, f32[4096]{0:T(1024)}, u32[]{:S(2)}) copy-start(f32[4096]{0:T(1024)} %param.20) | copy-start | bytes 49156
  48.4 88.2 %copy-start.43 = (f32[1024]{0:T(1024)S(1)}, f32[1024]{0:T(1024)}, u32[]{:S(2)}) copy-start(f32[1024]{0:T(1024)} %param.23) | copy-start | bytes 12292
  131.6 3.6 copy-start.18
  131.6 66.7 %copy-start.46 = (bf16[256,1024]{1,0:T(8,128)(2,1)S(1)}, bf16[256,1024]{1,0:T(8,128)(2,1)}, u32[]{:S(2)}) copy-start(bf16[256,1024]{1,0:T(8,128)(2,1)} %param.25) | copy-start | bytes 1572868
  131.6 66.7 %copy-start.47 = (f32[1024]{0:T(1024)S(1)}, f32[1024]{0:T(1024)}, u32[]{:S(2)}) copy-start(f32[1024]{0:T(1024)} %param.26) | copy-start | bytes 12292
  131.6 5.0 collective-permute-start.8
  137.0 64.8 %copy-start.26 = (bf16[128,1024]{1,0:T(8,128)(2,1)}, bf16[128,1024]{1,0:T(8,128)(2,1)S(1)}, u32[]{:S(2)}) copy-start(bf16[128,1024]{1,0:T(8,128)(2,1)S(1)} %multiply_convert_fusion.1) | copy-start | bytes 786436
  137.0 62.7 %copy-start.40 = (f32[16,1024]{1,0:T(8,128)S(1)}, f32[16,1024]{1,0:T(8,128)}, u32[]{:S(2)}) copy-start(f32[16,1024]{1,0:T(8,128)} %param.27) | copy-start | bytes 196612
  138.0 554.9 %all-gather.6.cloned.1.call-start = ((), (), s32[]{:S(2)}) async-start(), calls=%async_computation.6 | async-start | bytes 8912896 | tf_op jit(solution)/shard_map/all_gather | solution.py:108
  138.7 600.4 %reduce-scatter.3.cloned.1.call-start = ((), (), s32[]{:S(2)}) async-start(), calls=%async_computation.7 | async-start | bytes 1179648 | tf_op jit(solution)/shard_map/reduce_scatter | solution.py:111
  201.7 3.3 copy-start.3
  201.7 5.8 copy-start.2
  219.1 5.5 copy-start.7
  265.1 4.8 copy-start.23
  297.8 10.1 %copy-start.36 = (f32[1,16,1024]{2,1,0:T(8,128)S(1)}, f32[1,16,1024]{2,1,0:T(8,128)}, u32[]{:S(2)}) copy-start(f32[1,16,1024]{2,1,0:T(8,128)} %slice.347) | copy-start | bytes 196612
  320.4 4.2 copy-start.8
  327.6 5.0 copy-start.35
  334.2 18.6 %copy-start.16 = (f32[32,16,1024]{2,1,0:T(8,128)S(1)}, f32[32,16,1024]{2,1,0:T(8,128)}, u32[]{:S(2)}) copy-start(f32[32,16,1024]{2,1,0:T(8,128)} %add.271) | copy-start | bytes 6291460
  371.6 35.6 %copy-start.17 = (f32[31,16,1024]{2,1,0:T(8,128)S(1)}, f32[31,16,1024]{2,1,0:T(8,128)}, u32[]{:S(2)}) copy-start(f32[31,16,1024]{2,1,0:T(8,128)} %get-tuple-element.56) | copy-start | bytes 6094852
  371.6 35.6 %copy-start.34 = (f32[1,16,1024]{2,1,0:T(8,128)S(1)}, f32[1,16,1024]{2,1,0:T(8,128)}, u32[]{:S(2)}) copy-start(f32[1,16,1024]{2,1,0:T(8,128)} %slice.369) | copy-start | bytes 196612
  408.7 18.6 %copy-start.15 = (f32[32,16,1024]{2,1,0:T(8,128)S(1)}, f32[32,16,1024]{2,1,0:T(8,128)}, u32[]{:S(2)}) copy-start(f32[32,16,1024]{2,1,0:T(8,128)} %add.280) | copy-start | bytes 6291460
  439.2 7.1 copy-start.4
  439.2 7.1 copy-start.5
  439.2 8.6 copy-start.6
  447.8 7.5 copy-start.33
  493.4 35.5 %copy-start.32 = (f32[1,16,1024]{2,1,0:T(8,128)S(1)}, f32[1,16,1024]{2,1,0:T(8,128)}, u32[]{:S(2)}) copy-start(f32[1,16,1024]{2,1,0:T(8,128)} %slice.368) | copy-start | bytes 196612
  569.3 109.5 %copy-start.31 = (f32[128,16]{1,0:T(8,128)S(1)}, f32[128,16]{1,0:T(8,128)}, u32[]{:S(2)}) copy-start(f32[128,16]{1,0:T(8,128)} %copy.42) | copy-start | bytes 24580
  571.1 5.0 collective-permute-start
  576.2 5.8 collective-permute-start
  582.0 6.0 collective-permute-start
  588.0 5.8 collective-permute-start
  593.8 5.8 collective-permute-start
  599.7 7.1 collective-permute-start
  606.8 8.1 collective-permute-start
  614.9 8.1 collective-permute-start
  623.0 7.9 collective-permute-start
  630.9 7.9 collective-permute-start
  638.9 8.0 collective-permute-start
  646.9 7.8 collective-permute-start
  654.8 8.0 collective-permute-start
  662.7 8.1 collective-permute-start
  670.9 7.9 collective-permute-start
  678.8 14.1 %copy-start.19 = (f32[128,2,1024]{2,0,1:T(8,128)S(1)}, f32[128,2,1024]{2,0,1:T(8,128)}, u32[]{:S(2)}) copy-start(f32[128,2,1024]{2,0,1:T(8,128)} %copy-done.18) | copy-start | bytes 3145732
  678.8 14.1 %copy-start.27 = (bf16[128,1024]{1,0:T(8,128)(2,1)S(1)}, bf16[128,1024]{1,0:T(8,128)(2,1)}, u32[]{:S(2)}) copy-start(bf16[128,1024]{1,0:T(8,128)(2,1)} %copy-done.26) | copy-start | bytes 786436
  678.8 14.1 %copy-start.48 = (f32[1024]{0:T(1024)S(1)}, f32[1024]{0:T(1024)}, u32[]{:S(2)}) copy-start(f32[1024]{0:T(1024)} %param.28) | copy-start | bytes 12292
  692.8 5.9 copy-start.44
  692.8 47.4 %copy-start.42 = (f32[4096]{0:T(1024)S(1)}, f32[4096]{0:T(1024)}, u32[]{:S(2)}) copy-start(f32[4096]{0:T(1024)} %param.30) | copy-start | bytes 49156
  698.6 90.3 %all-gather.8.cloned.1.call-start = ((), (), s32[]{:S(2)}) async-start(), calls=%async_computation.8 | async-start | bytes 4718592 | tf_op jit(solution)/shard_map/all_gather | solution.py:131
  759.5 94.1 %reduce-scatter.5.cloned.1.call-start = ((), (), s32[]{:S(2)}) async-start(), calls=%async_computation.9 | async-start | bytes 4718592 | tf_op jit(solution)/shard_map/reduce_scatter | solution.py:137
  815.6 47.2 %copy-start.45 = (f32[16,2]{0,1:T(2,128)S(1)}, f32[16,2]{0,1:T(2,128)}, u32[]{:S(2)}) copy-start(f32[16,2]{0,1:T(2,128)} %param.32) | copy-start | bytes 388
  815.6 57.4 %copy-start.25 = (bf16[16,4096]{1,0:T(8,128)(2,1)S(1)}, bf16[16,4096]{1,0:T(8,128)(2,1)}, u32[]{:S(2)}) copy-start(bf16[16,4096]{1,0:T(8,128)(2,1)} %reduce-scatter.3.cloned.1.call-done) | copy-start | bytes 393220
  815.6 58.4 %copy-start.1 = (bf16[1024,288]{0,1:T(8,128)(2,1)S(1)}, bf16[1024,288]{0,1:T(8,128)(2,1)}, u32[]{:S(2)}) copy-start(bf16[1024,288]{0,1:T(8,128)(2,1)} %param.24) | copy-start | bytes 1769476
  855.7 17.2 %all-to-all-start.1 = ((bf16[16,4,4096]{2,1,0:T(4,128)(2,1)}), bf16[16,4,4096]{2,1,0:T(4,128)(2,1)S(1)}, u32[]{:S(2)}, u32[]{:S(2)}) async-start(bf16[16,4,4096]{2,1,0:T(4,128)(2,1)} %reshape.81), calls=%async_computation.3 | async-start | bytes 1048576 | tf_op jit(solution)/shard_map/all_to_all | solution.py:143
  (15 other events, 28.1 us)
Sparse Core Ops, SparseCore 0:
  9.5 113.8 all-gather.3
  138.1 60.1 all-reduce.29
  200.6 77.5 all-gather.5
  698.7 40.3 reduce-scatter.2
  759.6 29.1 all-gather.7
  815.7 37.8 reduce-scatter.4
